TPU v7x, 32 devices: a whole 2x2x4 slice. The times are simulated.
32 devices in a mesh: lag: 4 (over z), probe: 4 (over y, x), sketch: 2 (over core).
Axes of the slice: x: 2, y: 2, z: 4, core: 2. Of those that a mesh axis runs over, the one named last changes fastest.
Arguments:
- markov: bfloat16 [16, 32, 8192], P('lag', None, ('probe', 'sketch')), may hold values from -36 to 36
- test_matrix: bfloat16 [4, 32, 256], P('lag', None, 'sketch'), may hold values from -0.5 to 0.5
Outputs:
- sketch_out: bfloat16 [16, 8192, 256], P('lag', 'probe', 'sketch')
All inputs are finite; a program needn't handle non-finite values.
Results may differ from a plain program's by a relative error of at most 0.0004.
Values may be sent and summed in bfloat16 or wider, within the bound.
A program may use at most 64 MiB of HBM per device.

v0:
```python
import jax
import jax.numpy as jnp
from jax import lax
from jax.sharding import PartitionSpec as P


def from_behind(block, axis, distance):
    devices = range(lax.axis_size(axis))
    route = [(i - distance, i) for i in devices if i - distance in devices]
    return lax.ppermute(block, axis, route)


def products(blocks, padded_matrix, first_block, block_count, step_count):
    input_count = blocks.shape[2]
    probe_count = blocks.shape[3]
    column_count = padded_matrix.shape[2]
    stacked = blocks.reshape(block_count * step_count * input_count, probe_count)
    parts_list = []
    for row_index in range(step_count):
        start_index = first_block * step_count + step_count - row_index
        sliced = lax.dynamic_slice_in_dim(padded_matrix, start_index, block_count * step_count, 0)
        parts_list.append(sliced.reshape(block_count * step_count * input_count, column_count))
    weights = jnp.concatenate(parts_list, axis=1)
    return lax.dot_general(
        stacked, weights, (((0,), (0,)), ((), ())), preferred_element_type=jnp.float32
    )


def local(markov, test_matrix):
    step_count = markov.shape[0]
    input_count = markov.shape[1]
    matrix_full = lax.all_gather(test_matrix, "lag", axis=0, tiled=True)
    lag_count = matrix_full.shape[0]
    column_count = matrix_full.shape[2]
    blocks_needed = (step_count + lag_count - 2) // step_count
    back_rows = (blocks_needed + 2) * step_count - lag_count
    padded_matrix = jnp.concatenate(
        [
            jnp.zeros((step_count, input_count, column_count), jnp.bfloat16),
            matrix_full,
            jnp.zeros((back_rows, input_count, column_count), jnp.bfloat16),
        ],
        axis=0,
    )
    travelling = lax.all_gather(markov, "sketch", axis=2, tiled=True)
    window = travelling[None]
    span_now = 1
    for level_bit in range((blocks_needed + 1).bit_length() - 1):
        window = jnp.concatenate([window, from_behind(window, "lag", -span_now)], axis=0)
        span_now = span_now * 2
    leftover = blocks_needed + 1 - span_now
    if leftover > 0:
        window = jnp.concatenate([window, from_behind(window[:leftover], "lag", -span_now)], axis=0)
    sketch_raw = products(window, padded_matrix, 0, blocks_needed + 1, step_count)
    probe_local = sketch_raw.shape[0]
    grouped = sketch_raw.reshape(probe_local, step_count, column_count)
    column_sums = lax.psum(jnp.sum(grouped * grouped, axis=(0, 1)), ("lag", "probe"))
    total_cells = step_count * lax.axis_size("lag") * probe_local * lax.axis_size("probe")
    factor = lax.rsqrt(column_sums / total_cells + 1e-06)
    return jnp.transpose(grouped * factor, (1, 0, 2)).astype(jnp.bfloat16)


def solution(mesh):
    return jax.shard_map(
        local,
        mesh=mesh,
        in_specs=(P("lag", None, ("probe", "sketch")), P("lag", None, "sketch")),
        out_specs=P("lag", "probe", "sketch"),
        check_vma=False,
    )
```

profile of v0, /device:TPU:0, one launch (start us, length us, event | category | flops | bytes accessed | tf_op | source)
XLA Modules:
  0.0 74.6 jit_solution(1511413148882737607)
XLA Ops:
  0.0 2.5 %all_gather.6 = bf16[4,32,2048]{2,1,0:T(8,128)(2,1)S(1)} all-gather(bf16[4,32,1024]{2,1,0:T(8,128)(2,1)} %param.2), channel_id=1, replica_groups=mesh['lag'=4,'probe'=4,'sketch'=2] {'sketch'}, dimensions={2}, use_global_device_ids=true | all-gather | bytes 786432 | tf_op jit(solution)/shard_map/all_gather | solution.py:45
  2.5 1.3 %collective-permute-start = (bf16[1,4,32,2048]{3,2,1,0:T(8,128)(2,1)S(1)}, bf16[1,4,32,2048]{3,2,1,0:T(8,128)(2,1)S(1)}, u32[]{:S(2)}, u32[]{:S(2)}) collective-permute-start(bf16[1,4,32,2048]{3,2,1,0:T(8,128)(2,1)S(1)} %bitcast.16), channel_id=1, source_target_pairs={{8,0},{16,8},{24,16},{9,1},{17,9},{25,17},{10,2},{18,10},{26,18},{... | collective-permute-start | bytes 1572872 | tf_op jit(solution)/shard_map/ppermute | solution.py:10
  3.8 0.1 pad.7.clone
  3.9 25.1 %all_gather.7 = bf16[4,32,128]{2,1,0:T(8,128)(2,1)S(1)} all-gather(bf16[1,32,128]{2,1,0:T(8,128)(2,1)} %param.3), channel_id=1, replica_groups=mesh['lag'=4,'probe'=4,'sketch'=2] {'lag'}, dimensions={0}, use_global_device_ids=true | all-gather | bytes 40960 | tf_op jit(solution)/shard_map/all_gather | solution.py:32
  29.0 0.1 maximum_maximum_fusion
  29.2 0.1 copy.8
  29.3 0.0 collective-permute-done
  29.3 0.1 pad_maximum_fusion
  29.5 3.1 %multiply_reduce_fusion = (f32[128]{0:T(128)S(1)}, f32[2048,4,128]{2,0,1:T(8,128)}) fusion(bf16[256,2048,1]{1,0,2:T(8,128)(2,1)S(1)} %bitcast.15, bf16[4,128,256]{2,1,0:T(8,128)(2,1)S(1)} %bitcast.18), kind=kOutput, calls=%fused_computation.1 | convolution fusion | flops 538967936 | bytes 5505536 | tf_op jit(solution)/shard_map/dot_general | solution.py:24
  32.6 38.2 %psum.7 = f32[128]{0:T(128)S(1)} all-reduce(f32[128]{0:T(128)S(1)} %get-tuple-element.8), channel_id=1, replica_groups=mesh['lag'=4,'probe'=4,'sketch'=2] {'lag','probe'}, use_global_device_ids=true, to_apply=%region_1.0 | all-reduce | flops 128 | bytes 1024 | tf_op jit(solution)/shard_map/psum | solution.py:57
  70.8 3.8 %fusion = bf16[4,2048,128]{2,1,0:T(8,128)(2,1)} fusion(f32[2048,4,128]{2,0,1:T(8,128)} %get-tuple-element.9, f32[128]{0:T(128)S(1)} %add_rsqrt_fusion), kind=kLoop, calls=%fused_computation.2 | loop fusion | flops 2097152 | bytes 6291968 | tf_op jit(solution)/shard_map/convert_element_type | solution.py:60
  (7 shorter events, 0.1 us)
Async XLA Ops:
  2.5 26.9 %collective-permute-start = (bf16[1,4,32,2048]{3,2,1,0:T(8,128)(2,1)S(1)}, bf16[1,4,32,2048]{3,2,1,0:T(8,128)(2,1)S(1)}, u32[]{:S(2)}, u32[]{:S(2)}) collective-permute-start(bf16[1,4,32,2048]{3,2,1,0:T(8,128)(2,1)S(1)} %bitcast.16), channel_id=1, source_target_pairs={{8,0},{16,8},{24,16},{9,1},{17,9},{25,17},{10,2},{18,10},{26,18},{... | collective-permute-start | bytes 1572872 | tf_op jit(solution)/shard_map/ppermute | solution.py:10
where the time goes:
time: 74.8 us; the launch traced here: 74.6 us
  blocking collectives  65.8 us (88%)
  other arithmetic  4.08 us (5%)
  matrix products  3.13 us (4%)
  starting transfers between devices  1.28 us (2%)
    psum x1, blocking collectives, local(): lax.psum(jnp.sum(grouped * grouped, axis=(0, 1)), ('lag', 'probe'))  38.2 us
    all_gather x1, blocking collectives, local(): matrix_full = lax.all_gather(test_matrix, 'lag', axis=0, tiled=True)  25.1 us
    convert_element_type x1, other arithmetic, local(): return jnp.transpose(grouped * factor, (1, 0, 2)).astype(jnp.bfloat16)  3.84 us
    dot_general x1, matrix products, products(): lax.dot_general(stacked, weights, (((0,), (0,)), ((), ())), preferred_ele...  3.13 us
    all_gather x1, blocking collectives, local(): travelling = lax.all_gather(markov, 'sketch', axis=2, tiled=True)  2.46 us
  transfers between devices with their start and end apart: 1, of which 0 were waited for; matrix products, arithmetic and copies ran while one was open for 1% of the time, Pallas kernels for 0%

commit v1 on v0

v1 whole, which is shorter than its diff:
```python
import functools

import jax
import jax.numpy as jnp
from jax import lax
from jax.experimental import pallas as pl
from jax.experimental.pallas import tpu as pltpu
from jax.sharding import PartitionSpec as P

MESH = pl.DeviceIdType.MESH
UNROLL = 32


def loop(count, body):
    if count <= UNROLL:
        for index in range(count):
            body(index)
    else:
        def step(index, carry):
            body(index)
            return carry
        lax.fori_loop(0, count, step, 0)


def plan(step_count, lag_total):
    steps = step_count + lag_total - 1
    blocks = (steps - 1) // step_count
    pieces = []
    for ahead in range(1, blocks + 1):
        used = min(step_count, steps - ahead * step_count)
        if blocks == 1:
            pieces += [(ahead, at, 1) for at in range(used)]
        else:
            pieces.append((ahead, 0, used))
    return steps, pieces


def gather_kernel(
    sizes, markov, matrix, raw, factor,
    window, held, weights, sums,
    own_sem, matrix_own_sem, matrix_send, matrix_recv,
    pair_send, pair_recv, lag_send, lag_recv, next_send, next_recv, sum_send, sum_recv,
):
    n_lag, n_probe, n_sketch = sizes
    step_count, input_count, half = markov.shape
    matrix_rows = matrix.shape[0]
    columns = matrix.shape[2]
    lag_total = matrix_rows * n_lag
    steps, pieces = plan(step_count, lag_total)
    lag = lax.axis_index("lag")
    probe = lax.axis_index("probe")
    sketch = lax.axis_index("sketch")
    flat = lag * n_probe + probe
    peers = n_lag * n_probe - 1

    def peer(index):
        other = lax.rem(flat + 1 + index, peers + 1)
        return {
            "lag": lax.div(other, n_probe),
            "probe": lax.rem(other, n_probe),
            "sketch": sketch,
        }

    def partner(index):
        return {"lag": lag, "probe": probe, "sketch": lax.rem(sketch + 1 + index, n_sketch)}

    def lag_peer(index):
        return {"lag": lax.rem(lag + 1 + index, n_lag), "probe": probe, "sketch": sketch}

    barrier = pltpu.get_barrier_semaphore()

    def greet(index):
        pl.semaphore_signal(barrier, inc=1, device_id=peer(index), device_id_type=MESH)

    for index in range(n_sketch - 1):
        pl.semaphore_signal(barrier, inc=1, device_id=partner(index), device_id_type=MESH)
    loop(peers, greet)

    own = pltpu.make_async_copy(markov, window.at[sketch, pl.ds(0, step_count)], own_sem)
    own.start()
    matrix_own = pltpu.make_async_copy(
        matrix, held.at[pl.ds(lag * matrix_rows, matrix_rows)], matrix_own_sem
    )
    matrix_own.start()
    weights[...] = jnp.zeros_like(weights)
    for ahead, at, count in pieces:
        @pl.when(lag + ahead >= n_lag)
        def _():
            place = pl.ds(ahead * step_count + at, count)
            window[:, place] = jnp.zeros((n_sketch, count, input_count, half), window.dtype)

    pl.semaphore_wait(barrier, peers + n_sketch - 1)

    def lag_copy(number):
        ahead, at, count = pieces[number]
        return pltpu.make_async_remote_copy(
            src_ref=markov.at[pl.ds(at, count)],
            dst_ref=window.at[sketch, pl.ds(ahead * step_count + at, count)],
            send_sem=lag_send.at[number],
            recv_sem=lag_recv.at[number],
            device_id={"lag": lax.max(lag - ahead, 0), "probe": probe, "sketch": sketch},
            device_id_type=MESH,
        )

    def pair_copy(index):
        return pltpu.make_async_remote_copy(
            src_ref=markov,
            dst_ref=window.at[sketch, pl.ds(0, step_count)],
            send_sem=pair_send.at[index],
            recv_sem=pair_recv.at[index],
            device_id=partner(index),
            device_id_type=MESH,
        )

    def next_copy(number, index):
        ahead, at, count = pieces[number]
        place = window.at[sketch, pl.ds(ahead * step_count + at, count)]
        return pltpu.make_async_remote_copy(
            src_ref=place,
            dst_ref=place,
            send_sem=next_send.at[number, index],
            recv_sem=next_recv.at[number, index],
            device_id=partner(index),
            device_id_type=MESH,
        )

    def matrix_copy(index):
        return pltpu.make_async_remote_copy(
            src_ref=matrix,
            dst_ref=held.at[pl.ds(lag * matrix_rows, matrix_rows)],
            send_sem=matrix_send,
            recv_sem=matrix_recv,
            device_id=lag_peer(index),
            device_id_type=MESH,
        )

    for number in range(len(pieces)):
        @pl.when(lag >= pieces[number][0])
        def _():
            lag_copy(number).start()
        if number == 0:
            loop(n_lag - 1, lambda index: matrix_copy(index).start())
            for index in range(n_sketch - 1):
                pair_copy(index).start()

    matrix_own.wait()
    if n_lag > 1:
        arrived = held.at[pl.ds(0, (n_lag - 1) * matrix_rows)]
        pltpu.make_async_copy(arrived, arrived, matrix_recv).wait()
        pltpu.make_async_copy(arrived, arrived, matrix_send).wait()
    for row in range(step_count):
        weights[pl.ds(row * input_count, lag_total * input_count), row * columns:(row + 1) * columns] = (
            held[...].reshape(lag_total * input_count, columns)
        )

    def forward(number):
        @pl.when(lag + pieces[number][0] < n_lag)
        def _():
            lag_copy(number).wait_recv()
            for index in range(n_sketch - 1):
                next_copy(number, index).start()

    def landed(number):
        @pl.when(lag + pieces[number][0] < n_lag)
        def _():
            for index in range(n_sketch - 1):
                next_copy(number, index).wait()

    tile = min(256, half)
    group = 2 if step_count % 2 == 0 else 1

    def compute(first, total):
        depth = (lag_total + group - 1) * input_count
        weight = weights[pl.ds(first * input_count, depth), first * columns:(first + group) * columns]
        for side in range(n_sketch):
            def body(at, total):
                start = pl.multiple_of(at * tile, tile)
                block = window[side, pl.ds(first, lag_total + group - 1), :, pl.ds(start, tile)]
                product = lax.dot_general(
                    block.reshape(depth, tile), weight, (((0,), (0,)), ((), ())),
                    preferred_element_type=jnp.float32,
                )
                for row in range(group):
                    part = product[:, row * columns:(row + 1) * columns]
                    raw[first + row, pl.ds(side * half + start, tile), :] = part
                    total = total + jnp.sum((part * part).reshape(tile // 8, 8, columns), axis=0)
                return total
            total = lax.fori_loop(0, half // tile, body, total, unroll=depth <= 512)
        return total

    own.wait()
    total = jnp.zeros((8, columns), jnp.float32)
    done = 0
    paired = False
    for first in range(0, step_count, group):
        need = first + group - 1 + lag_total
        ready = done
        while ready < len(pieces) and pieces[ready][0] * step_count + pieces[ready][1] < need:
            forward(ready)
            ready += 1
        if not paired:
            for index in range(n_sketch - 1):
                pair_copy(index).wait()
            paired = True
        for number in range(done, ready):
            landed(number)
        done = ready
        total = compute(first, total)

    sums[pl.ds(flat, 1), :] = jnp.sum(total, axis=0, keepdims=True)

    def sum_copy(index):
        place = sums.at[pl.ds(flat, 1)]
        return pltpu.make_async_remote_copy(
            src_ref=place,
            dst_ref=place,
            send_sem=sum_send,
            recv_sem=sum_recv,
            device_id=peer(index),
            device_id_type=MESH,
        )

    loop(peers, lambda index: sum_copy(index).start())
    for number in range(len(pieces)):
        @pl.when(lag >= pieces[number][0])
        def _():
            lag_copy(number).wait_send()
    if peers:
        arrived = sums.at[pl.ds(0, peers)]
        pltpu.make_async_copy(arrived, arrived, sum_recv).wait()
        pltpu.make_async_copy(arrived, arrived, sum_send).wait()
    cells = step_count * n_lag * half * n_sketch * n_probe
    mean = jnp.sum(sums[...], axis=0, keepdims=True) / cells
    factor[...] = jnp.broadcast_to(lax.rsqrt(mean + 1e-06), factor.shape)


def local(sizes, markov, test_matrix):
    n_lag, n_probe, n_sketch = sizes
    step_count, input_count, half = markov.shape
    matrix_rows, _, columns = test_matrix.shape
    lag_total = matrix_rows * n_lag
    steps, pieces = plan(step_count, lag_total)
    count = max(len(pieces), 1)
    pairs = max(n_sketch - 1, 1)
    probes = half * n_sketch
    dma = pltpu.SemaphoreType.DMA
    raw, factor = pl.pallas_call(
        functools.partial(gather_kernel, sizes),
        out_shape=[
            pltpu.VMEM((step_count, probes, columns), jnp.float32),
            pltpu.VMEM((8, columns), jnp.float32),
        ],
        in_specs=[pl.BlockSpec(memory_space=pltpu.HBM)] * 2,
        out_specs=[pl.BlockSpec(memory_space=pltpu.VMEM)] * 2,
        scratch_shapes=[
            pltpu.VMEM((n_sketch, steps, input_count, half), jnp.bfloat16),
            pltpu.VMEM((lag_total, input_count, columns), jnp.bfloat16),
            pltpu.VMEM((steps * input_count, step_count * columns), jnp.bfloat16),
            pltpu.VMEM((n_lag * n_probe, columns), jnp.float32),
            dma, dma, dma, dma,
            dma((pairs,)), dma((pairs,)),
            dma((count,)), dma((count,)),
            dma((count, pairs)), dma((count, pairs)),
            dma, dma,
        ],
        compiler_params=pltpu.CompilerParams(
            collective_id=0, has_side_effects=True, vmem_limit_bytes=40 * 1024 * 1024
        ),
    )(markov, test_matrix)
    return (raw * factor[0]).astype(jnp.bfloat16)


def solution(mesh):
    sizes = tuple(mesh.shape[name] for name in ("lag", "probe", "sketch"))
    return jax.shard_map(
        functools.partial(local, sizes),
        mesh=mesh,
        in_specs=(P("lag", None, ("probe", "sketch")), P("lag", None, "sketch")),
        out_specs=P("lag", "probe", "sketch"),
        check_vma=False,
    )
```

time: 74.8 us -> 20.2 us (0.27)
  blocking collectives: 65.8 us -> 0 us
  Pallas kernels: 0 us -> 16.7 us
  matrix products: 3.13 us -> 0 us
  other arithmetic: 4.08 us -> 1.65 us
  local copies, waits for them, and re-layouts: 0.26 us -> 1.65 us
  starting transfers between devices: 1.28 us -> 0 us
    psum x1 -> x0, blocking collectives: 38.2 us -> none  [local(): lax.psum(jnp.sum(grouped * grouped, axis=(0, 1)), ('lag', 'probe'))]
    all_gather x2 -> x0, blocking collectives: 27.6 us -> none  [the longest x1 25.1 us: local(): matrix_full = lax.all_gather(test_matrix, 'lag', axis=0, tiled=True)]
    pallas_call x0 -> x1, Pallas kernels: none -> 16.7 us  [local(): pl.pallas_call(functools.partial(gather_kernel, sizes), out_shape=[pltpu....]
    dot_general x1 -> x0, matrix products: 3.13 us -> none  [products(): lax.dot_general(stacked, weights, (((0,), (0,)), ((), ())), preferred_ele...]
    convert_element_type x1, other arithmetic: 3.84 us -> 1.65 us  [local(): return (raw * factor[0]).astype(jnp.bfloat16)]
    unnamed x0 -> x4, local copies, waits for them, and re-layouts: none -> 1.65 us
    ppermute x1 -> x0, starting transfers between devices: 1.28 us -> none  [from_behind(): return lax.ppermute(block, axis, route)]
  transfers between devices with their start and end apart: 1 -> 0, of which waited for: 0 -> 0; matrix products, arithmetic and copies ran while one was open for 1% -> 0% of each run, Pallas kernels for 0% -> 0%
where the time goes in v1:
time: 20.2 us; the launch traced here: 20 us
  Pallas kernels  16.7 us (83%)
  local copies, waits for them, and re-layouts  1.65 us (8%)
  other arithmetic  1.65 us (8%)
    pallas_call x1, Pallas kernels, local(): pl.pallas_call(functools.partial(gather_kernel, sizes), out_shape=[pltpu....  16.7 us
    convert_element_type x1, other arithmetic, local(): return (raw * factor[0]).astype(jnp.bfloat16)  1.65 us
    unnamed x4, local copies, waits for them, and re-layouts  1.65 us

profile of v1, /device:TPU:0, one launch (start us, length us, event | category | flops | bytes accessed | tf_op | source)
XLA Modules:
  0.0 20.0 jit_solution(10623578970454018445)
XLA Ops:
  0.0 0.0 copy-start
  0.0 0.9 %copy-done = bf16[4,32,1024]{2,1,0:T(8,128)(2,1)S(1)} copy-done((bf16[4,32,1024]{2,1,0:T(8,128)(2,1)S(1)}, bf16[4,32,1024]{2,1,0:T(8,128)(2,1)}, u32[]{:S(2)}) %copy-start) | copy-done | bytes 262168
  1.0 0.0 copy-start.1
  1.0 0.7 %copy-done.1 = bf16[1,32,128]{2,1,0:T(8,128)(2,1)S(1)} copy-done((bf16[1,32,128]{2,1,0:T(8,128)(2,1)S(1)}, bf16[1,32,128]{2,1,0:T(8,128)(2,1)}, u32[]{:S(2)}) %copy-start.1) | copy-done | bytes 8216
  1.6 16.7 %shard_map.28 = (f32[4,2048,128]{2,1,0:T(8,128)S(1)}, f32[8,128]{1,0:T(8,128)S(1)}) custom-call(bf16[4,32,1024]{2,1,0:T(8,128)(2,1)S(1)} %copy-done, bf16[1,32,128]{2,1,0:T(8,128)(2,1)S(1)} %copy-done.1), custom_call_target="tpu_custom_call" | custom-call | tf_op jit(solution)/shard_map/pallas_call | solution.py:247
  18.4 1.6 %multiply_convert_fusion = bf16[4,2048,128]{2,1,0:T(8,128)(2,1)} fusion(f32[4,2048,128]{2,1,0:T(8,128)S(1)} %get-tuple-element.7, f32[128]{0:T(128)S(1)} %slice_bitcast_fusion), kind=kLoop, calls=%fused_computation | loop fusion | flops 2097152 | bytes 6291968 | tf_op jit(solution)/shard_map/convert_element_type | solution.py:270
  (1 shorter events, 0.0 us)
Async XLA Ops:
  0.0 0.9 %copy-start = (bf16[4,32,1024]{2,1,0:T(8,128)(2,1)S(1)}, bf16[4,32,1024]{2,1,0:T(8,128)(2,1)}, u32[]{:S(2)}) copy-start(bf16[4,32,1024]{2,1,0:T(8,128)(2,1)} %markov.1) | copy-start | bytes 786436
  1.0 0.7 %copy-start.1 = (bf16[1,32,128]{2,1,0:T(8,128)(2,1)S(1)}, bf16[1,32,128]{2,1,0:T(8,128)(2,1)}, u32[]{:S(2)}) copy-start(bf16[1,32,128]{2,1,0:T(8,128)(2,1)} %matrix.1) | copy-start | bytes 24580

commit v2 on v1

--- a/solution.py
+++ b/solution.py
@@ -232,6 +232,40 @@
     cells = step_count * n_lag * half * n_sketch * n_probe
     mean = jnp.sum(sums[...], axis=0, keepdims=True) / cells
     factor[...] = jnp.broadcast_to(lax.rsqrt(mean + 1e-06), factor.shape)
+
+
+def scale_kernel(raw, factor, out, held, sem):
+    step_count, probes, columns = raw.shape
+    pieces = 2
+    part = probes // pieces
+    copies = []
+    gain = factor[0:1, :]
+    for row in range(step_count):
+        for piece in range(pieces):
+            place = pl.ds(piece * part, part)
+            held[row, place] = (raw[row, place] * gain).astype(held.dtype)
+            copy = pltpu.make_async_copy(
+                held.at[row, place], out.at[row, place], sem.at[row * pieces + piece]
+            )
+            copy.start()
+            copies.append(copy)
+    for copy in copies:
+        copy.wait()
+
+
+def scale(raw, factor):
+    step_count, probes, columns = raw.shape
+    return pl.pallas_call(
+        scale_kernel,
+        out_shape=jax.ShapeDtypeStruct(raw.shape, jnp.bfloat16),
+        in_specs=[pl.BlockSpec(memory_space=pltpu.VMEM)] * 2,
+        out_specs=pl.BlockSpec(memory_space=pltpu.HBM),
+        scratch_shapes=[
+            pltpu.VMEM(raw.shape, jnp.bfloat16),
+            pltpu.SemaphoreType.DMA((step_count * 2,)),
+        ],
+        compiler_params=pltpu.CompilerParams(vmem_limit_bytes=16 * 1024 * 1024),
+    )(raw, factor)
 
 
 def local(sizes, markov, test_matrix):
@@ -264,10 +298,10 @@
             dma, dma,
         ],
         compiler_params=pltpu.CompilerParams(
-            collective_id=0, has_side_effects=True, vmem_limit_bytes=40 * 1024 * 1024
+            collective_id=0, has_side_effects=True, vmem_limit_bytes=59 * 1024 * 1024
         ),
     )(markov, test_matrix)
-    return (raw * factor[0]).astype(jnp.bfloat16)
+    return scale(raw, factor)
 
 
 def solution(mesh):

time: 20.2 us -> 18.5 us (0.916)
  other arithmetic: 1.65 us -> 0 us
  local copies, waits for them, and re-layouts: 1.65 us -> 0 us
  Pallas kernels: 16.7 us -> 18.3 us
    convert_element_type x1 -> x0, other arithmetic: 1.65 us -> none  [local(): return (raw * factor[0]).astype(jnp.bfloat16)]
    unnamed x4 -> x0, local copies, waits for them, and re-layouts: 1.65 us -> none
    pallas_call x0 -> x1, Pallas kernels: none -> 1.41 us  [scale(): pl.pallas_call(scale_kernel, out_shape=jax.ShapeDtypeStruct(raw.shape, jn...]
    pallas_call x1, Pallas kernels: 16.7 us -> 16.9 us  [local(): pl.pallas_call(functools.partial(gather_kernel, sizes), out_shape=[pltpu....]
where the time goes in v2:
time: 18.5 us; the launch traced here: 18.3 us
  Pallas kernels  18.3 us (99%)
    pallas_call x1, Pallas kernels, local(): pl.pallas_call(functools.partial(gather_kernel, sizes), out_shape=[pltpu....  16.9 us
    pallas_call x1, Pallas kernels, scale(): pl.pallas_call(scale_kernel, out_shape=jax.ShapeDtypeStruct(raw.shape, jn...  1.41 us

profile of v2, /device:TPU:0, one launch (start us, length us, event | category | flops | bytes accessed | tf_op | source)
XLA Modules:
  0.0 18.3 jit_solution(9878859147490770587)
XLA Ops:
  0.0 16.9 %shard_map.28 = (f32[4,2048,128]{2,1,0:T(8,128)S(1)}, f32[8,128]{1,0:T(8,128)S(1)}) custom-call(bf16[4,32,1024]{2,1,0:T(8,128)(2,1)} %markov.1, bf16[1,32,128]{2,1,0:T(8,128)(2,1)} %matrix.1), custom_call_target="tpu_custom_call" | custom-call | tf_op jit(solution)/shard_map/pallas_call | solution.py:281
  16.9 1.4 %shard_map.29 = bf16[4,2048,128]{2,1,0:T(8,128)(2,1)} custom-call(f32[4,2048,128]{2,1,0:T(8,128)S(1)} %get-tuple-element.7.raw, f32[8,128]{1,0:T(8,128)S(1)} %get-tuple-element.8.factor), custom_call_target="tpu_custom_call" | custom-call | tf_op jit(solution)/shard_map/pallas_call | solution.py:258

commit v3 on v2

--- a/solution.py
+++ b/solution.py
@@ -9,6 +9,7 @@
 
 MESH = pl.DeviceIdType.MESH
 UNROLL = 32
+TILES = 4
 
 
 def loop(count, body):
@@ -134,14 +135,17 @@
             device_id_type=MESH,
         )
 
-    for number in range(len(pieces)):
+    loop(n_lag - 1, lambda index: matrix_copy(index).start())
+    for number in range(0, 1):
         @pl.when(lag >= pieces[number][0])
         def _():
             lag_copy(number).start()
-        if number == 0:
-            loop(n_lag - 1, lambda index: matrix_copy(index).start())
-            for index in range(n_sketch - 1):
-                pair_copy(index).start()
+    for index in range(n_sketch - 1):
+        pair_copy(index).start()
+    for number in range(1, len(pieces)):
+        @pl.when(lag >= pieces[number][0])
+        def _():
+            lag_copy(number).start()
 
     matrix_own.wait()
     if n_lag > 1:
@@ -268,11 +272,298 @@
     )(raw, factor)
 
 
+def mirror_kernel(
+    sizes, markov, matrix, raw, factor,
+    window, held, weights, acc, sums,
+    own_sem, matrix_own_sem, matrix_send, matrix_recv,
+    pair_send, pair_recv, down_send, down_recv, up_send, up_recv,
+    down_pair_send, down_pair_recv, up_pair_send, up_pair_recv,
+    sum_send, sum_recv, known,
+):
+    n_lag, n_probe, n_sketch = sizes
+    step_count, input_count, half = markov.shape
+    matrix_rows = matrix.shape[0]
+    columns = matrix.shape[2]
+    lag_total = matrix_rows * n_lag
+    tail = lag_total - 1
+    alone = step_count - tail
+    tile = half // TILES
+    early = TILES // 2
+    lag = lax.axis_index("lag")
+    probe = lax.axis_index("probe")
+    sketch = lax.axis_index("sketch")
+    flat = lag * n_probe + probe
+    peers = n_lag * n_probe - 1
+    has_next = lag < n_lag - 1
+    has_back = lag > 0
+
+    def peer(index):
+        other = lax.rem(flat + 1 + index, peers + 1)
+        return {
+            "lag": lax.div(other, n_probe),
+            "probe": lax.rem(other, n_probe),
+            "sketch": sketch,
+        }
+
+    def partner(index):
+        return {"lag": lag, "probe": probe, "sketch": lax.rem(sketch + 1 + index, n_sketch)}
+
+    def lag_peer(index):
+        return {"lag": lax.rem(lag + 1 + index, n_lag), "probe": probe, "sketch": sketch}
+
+    def probe_peer(index):
+        return {"lag": lag, "probe": lax.rem(probe + 1 + index, n_probe), "sketch": sketch}
+
+    barrier = pltpu.get_barrier_semaphore()
+    near = (
+        [partner(index) for index in range(n_sketch - 1)]
+        + [lag_peer(index) for index in range(n_lag - 1)]
+        + [probe_peer(index) for index in range(n_probe - 1)]
+    )
+    for device in near:
+        pl.semaphore_signal(barrier, inc=1, device_id=device, device_id_type=MESH)
+
+    own = pltpu.make_async_copy(markov, window.at[sketch, pl.ds(tail, step_count)], own_sem)
+    own.start()
+    matrix_own = pltpu.make_async_copy(
+        matrix, held.at[pl.ds(lag * matrix_rows, matrix_rows)], matrix_own_sem
+    )
+    matrix_own.start()
+    weights[...] = jnp.zeros_like(weights)
+    acc[...] = jnp.zeros_like(acc)
+
+    @pl.when(lag == n_lag - 1)
+    def _():
+        window[:, pl.ds(tail + step_count, tail)] = jnp.zeros(
+            (n_sketch, tail, input_count, half), window.dtype
+        )
+
+    pl.semaphore_wait(barrier, len(near))
+    for index in range(n_lag - 1):
+        pl.semaphore_signal(known, inc=1, device_id=lag_peer(index), device_id_type=MESH)
+
+    def spot(first, count, number):
+        return window.at[sketch, pl.ds(first, count), :, pl.ds(number * tile, tile)]
+
+    def remote(source, target, send, recv, device):
+        return pltpu.make_async_remote_copy(
+            src_ref=source, dst_ref=target, send_sem=send, recv_sem=recv,
+            device_id=device, device_id_type=MESH,
+        )
+
+    def down(number):
+        return remote(
+            markov.at[pl.ds(0, tail), :, pl.ds(number * tile, tile)],
+            spot(tail + step_count, tail, number),
+            down_send.at[number], down_recv.at[number],
+            {"lag": lax.max(lag - 1, 0), "probe": probe, "sketch": sketch},
+        )
+
+    def up(number):
+        return remote(
+            markov.at[pl.ds(alone, tail), :, pl.ds(number * tile, tile)],
+            spot(0, tail, number),
+            up_send.at[number], up_recv.at[number],
+            {"lag": lax.min(lag + 1, n_lag - 1), "probe": probe, "sketch": sketch},
+        )
+
+    def pair(index):
+        return remote(
+            markov, window.at[sketch, pl.ds(tail, step_count)],
+            pair_send.at[index], pair_recv.at[index], partner(index),
+        )
+
+    def down_pair(number, index):
+        place = spot(tail + step_count, tail, number)
+        return remote(
+            place, place, down_pair_send.at[number, index], down_pair_recv.at[number, index],
+            partner(index),
+        )
+
+    def up_pair(number, index):
+        place = spot(0, tail, number)
+        return remote(
+            place, place, up_pair_send.at[number, index], up_pair_recv.at[number, index],
+            partner(index),
+        )
+
+    def matrix_copy(index):
+        return remote(
+            matrix, held.at[pl.ds(lag * matrix_rows, matrix_rows)],
+            matrix_send, matrix_recv, lag_peer(index),
+        )
+
+    for index in range(n_lag - 1):
+        matrix_copy(index).start()
+
+    @pl.when(has_back)
+    def _():
+        for number in range(early):
+            down(number).start()
+
+    @pl.when(has_next)
+    def _():
+        for number in range(early, TILES):
+            up(number).start()
+
+    for index in range(n_sketch - 1):
+        pair(index).start()
+
+    @pl.when(has_back)
+    def _():
+        for number in range(early, TILES):
+            down(number).start()
+
+    matrix_own.wait()
+    arrived = held.at[pl.ds(0, (n_lag - 1) * matrix_rows)]
+    pltpu.make_async_copy(arrived, arrived, matrix_recv).wait()
+    pltpu.make_async_copy(arrived, arrived, matrix_send).wait()
+    for row in range(step_count):
+        weights[pl.ds(row * input_count, lag_total * input_count), row * columns:(row + 1) * columns] = (
+            held[...].reshape(lag_total * input_count, columns)
+        )
+
+    def compute(place, first, rows, side, start, width, stored, summed):
+        depth = (lag_total + rows - 1) * input_count
+        block = window[side, pl.ds(place, lag_total + rows - 1), :, pl.ds(start, width)]
+        product = lax.dot_general(
+            block.reshape(depth, width), weights[pl.ds(0, depth), 0:rows * columns],
+            (((0,), (0,)), ((), ())), preferred_element_type=jnp.float32,
+        )
+        total = jnp.zeros((8, columns), jnp.float32)
+        for row in range(rows):
+            part = product[:, row * columns:(row + 1) * columns]
+            if stored:
+                raw[first + row, pl.ds(side * half + start, width), :] = part
+            if summed:
+                total = total + jnp.sum((part * part).reshape(width // 8, 8, columns), axis=0)
+        if summed:
+            acc[...] += total
+
+    def forward_down(number):
+        @pl.when(has_next)
+        def _():
+            down(number).wait_recv()
+            for index in range(n_sketch - 1):
+                down_pair(number, index).start()
+
+    def forward_up(number):
+        @pl.when(has_back)
+        def _():
+            up(number).wait_recv()
+            for index in range(n_sketch - 1):
+                up_pair(number, index).start()
+
+    def own_rows(side, number, summed):
+        compute(tail + alone, alone, tail, side, number * tile, tile, True, summed)
+
+    own.wait()
+    for number in range(early):
+        forward_down(number)
+        forward_up(early + number)
+    for index in range(n_sketch - 1):
+        pair(index).wait()
+    for side in range(n_sketch):
+        for number in range(TILES):
+            compute(tail, 0, alone, side, number * tile, tile, True, True)
+    for number in range(early):
+        @pl.when(has_next)
+        def _():
+            for index in range(n_sketch - 1):
+                down_pair(number, index).wait()
+        for side in range(n_sketch):
+            own_rows(side, number, True)
+
+        @pl.when(has_back)
+        def _():
+            for index in range(n_sketch - 1):
+                up_pair(early + number, index).wait()
+            for side in range(n_sketch):
+                compute(0, alone, tail, side, (early + number) * tile, tile, False, True)
+
+    @pl.when(lag == n_lag - 1)
+    def _():
+        for side in range(n_sketch):
+            for number in range(early, TILES):
+                own_rows(side, number, True)
+
+    sums[pl.ds(flat, 1), :] = jnp.sum(acc[...], axis=0, keepdims=True)
+
+    def sum_copy(index):
+        place = sums.at[pl.ds(flat, 1)]
+        return remote(place, place, sum_send, sum_recv, peer(index))
+
+    pl.semaphore_wait(known, n_lag - 1)
+    for index in range(peers):
+        sum_copy(index).start()
+
+    for number in range(early, TILES):
+        forward_down(number)
+
+    @pl.when(has_next)
+    def _():
+        for number in range(early, TILES):
+            for index in range(n_sketch - 1):
+                down_pair(number, index).wait()
+            for side in range(n_sketch):
+                own_rows(side, number, False)
+        for number in range(early, TILES):
+            up(number).wait_send()
+
+    @pl.when(has_back)
+    def _():
+        for number in range(TILES):
+            down(number).wait_send()
+
+    arrived = sums.at[pl.ds(0, peers)]
+    pltpu.make_async_copy(arrived, arrived, sum_recv).wait()
+    pltpu.make_async_copy(arrived, arrived, sum_send).wait()
+    cells = step_count * n_lag * half * n_sketch * n_probe
+    mean = jnp.sum(sums[...], axis=0, keepdims=True) / cells
+    factor[...] = jnp.broadcast_to(lax.rsqrt(mean + 1e-06), factor.shape)
+
+
+def mirrored(sizes, markov, test_matrix):
+    n_lag, n_probe, n_sketch = sizes
+    step_count, input_count, half = markov.shape
+    matrix_rows, _, columns = test_matrix.shape
+    lag_total = matrix_rows * n_lag
+    tail = lag_total - 1
+    pairs = max(n_sketch - 1, 1)
+    dma = pltpu.SemaphoreType.DMA
+    return pl.pallas_call(
+        functools.partial(mirror_kernel, sizes),
+        out_shape=[
+            pltpu.VMEM((step_count, half * n_sketch, columns), jnp.float32),
+            pltpu.VMEM((8, columns), jnp.float32),
+        ],
+        in_specs=[pl.BlockSpec(memory_space=pltpu.HBM)] * 2,
+        out_specs=[pl.BlockSpec(memory_space=pltpu.VMEM)] * 2,
+        scratch_shapes=[
+            pltpu.VMEM((n_sketch, step_count + 2 * tail, input_count, half), jnp.bfloat16),
+            pltpu.VMEM((lag_total, input_count, columns), jnp.bfloat16),
+            pltpu.VMEM(((step_count + tail) * input_count, step_count * columns), jnp.bfloat16),
+            pltpu.VMEM((8, columns), jnp.float32),
+            pltpu.VMEM((n_lag * n_probe, columns), jnp.float32),
+            dma, dma, dma, dma,
+            dma((pairs,)), dma((pairs,)),
+            dma((TILES,)), dma((TILES,)), dma((TILES,)), dma((TILES,)),
+            dma((TILES, pairs)), dma((TILES, pairs)), dma((TILES, pairs)), dma((TILES, pairs)),
+            dma, dma, pltpu.SemaphoreType.REGULAR,
+        ],
+        compiler_params=pltpu.CompilerParams(
+            collective_id=1, has_side_effects=True, vmem_limit_bytes=59 * 1024 * 1024
+        ),
+    )(markov, test_matrix)
+
+
 def local(sizes, markov, test_matrix):
     n_lag, n_probe, n_sketch = sizes
     step_count, input_count, half = markov.shape
     matrix_rows, _, columns = test_matrix.shape
     lag_total = matrix_rows * n_lag
+    if 1 < lag_total <= step_count and n_lag > 1 and half % (128 * TILES) == 0:
+        return scale(*mirrored(sizes, markov, test_matrix))
     steps, pieces = plan(step_count, lag_total)
     count = max(len(pieces), 1)
     pairs = max(n_sketch - 1, 1)

time: 18.5 us -> 18.9 us (1.022)
  Pallas kernels: 18.3 us -> 18.8 us
    pallas_call x1, Pallas kernels: 16.9 us -> 17.4 us  [mirrored(): pl.pallas_call(functools.partial(mirror_kernel, sizes), out_shape=[pltpu....]
where the time goes in v3:
time: 18.9 us; the launch traced here: 18.8 us
  Pallas kernels  18.8 us (99%)
    pallas_call x1, Pallas kernels, mirrored(): pl.pallas_call(functools.partial(mirror_kernel, sizes), out_shape=[pltpu....  17.4 us
    pallas_call x1, Pallas kernels, scale(): pl.pallas_call(scale_kernel, out_shape=jax.ShapeDtypeStruct(raw.shape, jn...  1.41 us

profile of v3, /device:TPU:0, one launch (start us, length us, event | category | flops | bytes accessed | tf_op | source)
XLA Modules:
  0.0 18.8 jit_solution(414599736363660567)
XLA Ops:
  0.0 17.4 %shard_map.28 = (f32[4,2048,128]{2,1,0:T(8,128)S(1)}, f32[8,128]{1,0:T(8,128)S(1)}) custom-call(bf16[4,32,1024]{2,1,0:T(8,128)(2,1)} %markov.1, bf16[1,32,128]{2,1,0:T(8,128)(2,1)} %matrix.1), custom_call_target="tpu_custom_call" | custom-call | tf_op jit(solution)/shard_map/pallas_call | solution.py:534
  17.4 1.4 %shard_map.29 = bf16[4,2048,128]{2,1,0:T(8,128)(2,1)} custom-call(f32[4,2048,128]{2,1,0:T(8,128)S(1)} %get-tuple-element.7.raw, f32[8,128]{1,0:T(8,128)S(1)} %get-tuple-element.8.factor), custom_call_target="tpu_custom_call" | custom-call | tf_op jit(solution)/shard_map/pallas_call | solution.py:262
